TPU v7x, 256 devices: a whole 4x4x8 slice. The times are simulated.
256 devices in a mesh: exp: 64 (over z, y, core), voc: 4 (over x).
Axes of the slice: x: 4, y: 4, z: 8, core: 2. Of those that a mesh axis runs over, the one named last changes fastest.
Arguments:
- tokens: bfloat16 [2048, 4096], P('exp', 'voc'), may hold values from -6 to 6
- expert_routes: int32 [2048, 2], P('exp'), may hold values from 0 to 7, all different within a row; in each aligned block of 32 rows (0 to 31, 32 to 63, ...) at most 16 rows name the same one
- gate_scores: float32 [2048, 2], P('exp'), may hold values from 0.2 to 1
- w_gate: bfloat16 [64, 4096, 1792], P('exp', None, 'voc'), may hold values from -0.09375 to 0.09375
- w_up: bfloat16 [64, 4096, 1792], P('exp', None, 'voc'), may hold values from -0.09375 to 0.09375
- w_down: bfloat16 [64, 1792, 4096], P('exp', 'voc'), may hold values from -0.046875 to 0.046875
- head_weight: bfloat16 [4096, 32000], P('voc', 'exp'), may hold values from -0.09375 to 0.09375
- passage_ids: int32 [64, 32], replicated, may hold values from 0 to 3, never falling along the last dimension, each value on 1 to 16 neighbouring positions
- doc_length: int32 [64, 4], replicated, may hold values from 20 to 180, as said below
Outputs:
- term_scores: float32 [256, 32000], P('voc', 'exp')
Inputs may be any that keep to these rules, and one draw needn't show every extreme that they name: `expert_routes`: each row names 2 different experts; among the rows of one exp index (32 tokens) no expert is named more than 16 times. `passage_ids`: never falling along a row; every passage holds 1 to 16 tokens. `doc_length`: positive whole numbers of words.
All inputs are finite; a program needn't handle non-finite values.
Results may differ from a plain program's by a relative error of at most 0.0065.
Values may be sent and summed in bfloat16 or wider, within the bound.
A program may use at most 128 MiB of HBM per device.

v0:
```python
import jax
import jax.numpy as jnp
from jax import lax
from jax.sharding import PartitionSpec as P

EXPERTS = 8


def slot_tables(route_rows, gate_rows, capacity):
    count = route_rows.shape[0]
    expert_ids = jnp.arange(EXPERTS, dtype=jnp.int32)
    hit_table = (route_rows[:, :, None] == expert_ids).astype(jnp.int32)
    flat_hits = hit_table.reshape(count * 2, EXPERTS)
    rank_table = jnp.cumsum(flat_hits, axis=0) - flat_hits
    slot_table = jnp.sum(flat_hits * rank_table, axis=1).reshape(count, 2)
    slot_ids = jnp.arange(capacity, dtype=jnp.int32)
    matches = hit_table[:, :, :, None] * (slot_table[:, :, None, None] == slot_ids).astype(
        jnp.int32
    )
    place_table = jnp.sum(matches, axis=1)
    gate_table = jnp.sum(matches.astype(jnp.float32) * gate_rows[:, :, None, None], axis=1)
    return (place_table, gate_table)


def build_slots(place_table, token_rows, group_size):
    slot_rows = jnp.einsum(
        "tec,td->ecd",
        place_table.astype(jnp.bfloat16),
        token_rows,
        preferred_element_type=jnp.float32,
    ).astype(jnp.bfloat16)
    return jnp.repeat(slot_rows, group_size, axis=0)


def local(
    tokens, expert_routes, gate_scores, w_gate, w_up, w_down, head_weight, passage_ids, doc_length
):
    tok_count, width_slice = tokens.shape
    capacity = tok_count // 2
    exp_count = lax.axis_size("exp")
    voc_count = lax.axis_size("voc")
    group_size = exp_count // EXPERTS
    place_table, gate_table = slot_tables(expert_routes, gate_scores, capacity)
    gate_local = w_gate[0]
    up_local = w_up[0]
    down_local = w_down[0]
    slot_count = exp_count * capacity
    send_rows = build_slots(place_table, tokens, group_size)
    received = lax.all_to_all(send_rows, "exp", split_axis=0, concat_axis=0, tiled=True)
    received = received.reshape(slot_count, width_slice)
    block_rows = lax.all_gather(received, "voc", axis=1, tiled=True)
    gate_pre = jnp.dot(block_rows, gate_local, preferred_element_type=jnp.float32)
    up_pre = jnp.dot(block_rows, up_local, preferred_element_type=jnp.float32)
    hidden = (jax.nn.silu(gate_pre) * up_pre).astype(jnp.bfloat16)
    part = jnp.dot(hidden, down_local, preferred_element_type=jnp.float32)
    rounded = lax.optimization_barrier(part.astype(jnp.bfloat16)).astype(jnp.float32)
    rounded = rounded.reshape(exp_count, capacity, rounded.shape[1])
    summed = lax.psum_scatter(rounded.astype(jnp.bfloat16), "voc", scatter_dimension=2, tiled=True)
    returned = lax.all_to_all(summed, "exp", split_axis=0, concat_axis=0, tiled=True)
    member_sum = jnp.sum(
        returned.astype(jnp.float32).reshape(EXPERTS, group_size, capacity, width_slice), axis=1
    )
    moe = jnp.einsum("tec,ecd->td", gate_table, member_sum, precision=lax.Precision.HIGHEST)
    layer_out = (tokens.astype(jnp.float32) + moe).astype(jnp.bfloat16)
    gathered = lax.all_gather(layer_out, "exp", axis=0, tiled=True)
    logits = lax.psum_scatter(
        jnp.dot(gathered, head_weight, preferred_element_type=jnp.float32).astype(jnp.bfloat16),
        "voc",
        scatter_dimension=0,
        tiled=True,
    ).astype(jnp.float32)
    saturated = jnp.log1p(jnp.maximum(logits, 0.0))
    shards_here = exp_count // voc_count
    pass_count = doc_length.shape[1]
    first_shard = lax.axis_index("voc") * shards_here
    ids_here = lax.dynamic_slice_in_dim(passage_ids, first_shard, shards_here, 0)
    lengths_here = lax.dynamic_slice_in_dim(doc_length, first_shard, shards_here, 0)
    one_hot = (
        ids_here[:, None, :] == jnp.arange(pass_count, dtype=jnp.int32)[None, :, None]
    ).astype(jnp.float32)
    saturated = saturated.reshape(shards_here, tok_count, saturated.shape[1])
    freq = jnp.einsum("spt,stv->spv", one_hot, saturated, precision=lax.Precision.HIGHEST)
    avg_length = jnp.sum(doc_length.astype(jnp.float32)) / (doc_length.shape[0] * pass_count)
    scale = 1.0 - 0.75 + 0.75 * lengths_here.astype(jnp.float32) / avg_length
    scores = freq * (1.2 + 1.0) / (freq + 1.2 * scale[:, :, None])
    return scores.reshape(shards_here * pass_count, scores.shape[2])


def solution(mesh):
    in_specs = (
        P("exp", "voc"),
        P("exp", None),
        P("exp", None),
        P("exp", None, "voc"),
        P("exp", None, "voc"),
        P("exp", "voc", None),
        P("voc", "exp"),
        P(),
        P(),
    )
    out_specs = P("voc", "exp")
    return jax.shard_map(local, mesh=mesh, in_specs=in_specs, out_specs=out_specs, check_vma=False)
```

profile of v0, /device:TPU:1, one launch (start us, length us, event | category | flops | bytes accessed | tf_op | source)
XLA Modules:
  0.0 445.1 jit_solution(3002805824108448492)
XLA Ops:
  6.5 0.0 copy-start
  6.5 0.0 all-gather.3.cloned.1.call-start
  6.5 0.8 copy.23
  7.4 0.7 fusion.20
  8.1 0.1 eq.65
  8.2 0.1 fusion.16
  8.2 0.1 reduce_window_sum.11
  8.3 0.2 select_reduce_fusion
  8.5 0.1 eq.69
  8.6 0.1 copy.24
  8.8 1.0 convolution_convert_fusion.2
  9.8 0.3 broadcast_in_dim.2
  10.1 62.7 %all_to_all.10 = bf16[64,16,1024]{2,1,0:T(8,128)(2,1)} all-to-all(bf16[64,16,1024]{2,1,0:T(8,128)(2,1)S(1)} %bitcast.38), channel_id=1, replica_groups=mesh['exp'=64,'voc'=4] {'exp'}, dimensions={0} | all-to-all | bytes 4194304 | tf_op jit(solution)/shard_map/all_to_all | solution.py:49
  72.8 0.0 all-gather.3.cloned.1.call-update
  72.8 0.0 reduce-scatter.3.cloned.1.call-start
  72.9 83.4 %all-gather.3.cloned.1.call-done = bf16[1024,4096]{1,0:T(8,128)(2,1)} async-done(((bf16[1024,1024]{1,0:T(8,128)(2,1)}), bf16[1024,4096]{1,0:T(8,128)(2,1)}) %all-gather.3.cloned.1.call-update) | async-done | bytes 8388624 | tf_op jit(solution)/shard_map/all_gather | solution.py:51
  156.3 7.5 %fusion.3 = f32[1024,448]{0,1:T(8,128)S(1)} fusion(bf16[1024,4096]{1,0:T(8,128)(2,1)} %all-gather.3.cloned.1.call-done, bf16[1,4096,448]{1,2,0:T(8,128)(2,1)} %param.12), kind=kOutput, calls=%fused_computation.5 | convolution fusion | flops 3758096384 | bytes 13893632 | tf_op jit(solution)/shard_map/dot_general | solution.py:52
  163.8 15.2 %convolution_convert_fusion = bf16[1024,4096]{1,0:T(8,128)(2,1)} fusion(bf16[1,448,4096]{2,1,0:T(8,128)(2,1)} %param.14, f32[1024,448]{0,1:T(8,128)S(1)} %fusion.3, bf16[1024,4096]{1,0:T(8,128)(2,1)} %all-gather.3.cloned.1.call-done, bf16[1,4096,448]{1,2,0:T(8,128)(2,1)} %param.13), kind=kOutput, calls=%fused_computation | convolution fusion | flops 7523139584 | bytes 25952256 | tf_op jit(solution)/shard_map/dot_general | solution.py:55
  179.0 0.0 reduce-scatter.3.cloned.1.call-update
  179.1 0.0 copy-start.4
  179.1 0.0 copy-start.1
  179.1 84.3 %reduce-scatter.3.cloned.1.call-done = bf16[64,16,1024]{2,1,0:T(8,128)(2,1)} async-done(((bf16[64,16,4096]{2,1,0:T(8,128)(2,1)}), bf16[64,16,1024]{2,1,0:T(8,128)(2,1)}) %reduce-scatter.3.cloned.1.call-update) | async-done | bytes 2097168 | tf_op jit(solution)/shard_map/reduce_scatter | solution.py:58
  263.4 10.6 %all-to-all-start.1 = ((bf16[64,16,1024]{2,1,0:T(8,128)(2,1)}), bf16[64,16,1024]{2,1,0:T(8,128)(2,1)S(1)}, u32[]{:S(2)}, u32[]{:S(2)}) async-start(bf16[64,16,1024]{2,1,0:T(8,128)(2,1)} %reduce-scatter.3.cloned.1.call-done), calls=%async_computation.2 | async-start | bytes 4194304 | tf_op jit(solution)/shard_map/all_to_all | solution.py:59
  274.0 0.0 all-gather.5.cloned.1.call-start
  274.0 0.0 copy-done.4
  274.1 49.6 %all-to-all-done.1 = bf16[64,16,1024]{2,1,0:T(8,128)(2,1)S(1)} async-done(((bf16[64,16,1024]{2,1,0:T(8,128)(2,1)}), bf16[64,16,1024]{2,1,0:T(8,128)(2,1)S(1)}, u32[]{:S(2)}, u32[]{:S(2)}) %all-to-all-start.1) | async-done | bytes 2097184 | tf_op jit(solution)/shard_map/all_to_all | solution.py:59
  323.7 0.4 convert_reduce_fusion
  324.0 0.0 copy-done.1
  324.0 1.0 fusion.10
  325.1 0.0 all-gather.5.cloned.1.call-update
  325.1 0.0 copy-start.2
  325.1 0.0 copy-start.3
  325.1 0.2 reduce-scatter.5.cloned.1.call-start
  325.4 75.4 %all-gather.5.cloned.1.call-done = bf16[2048,1024]{1,0:T(8,128)(2,1)} async-done(((bf16[32,1024]{1,0:T(8,128)(2,1)}), bf16[2048,1024]{1,0:T(8,128)(2,1)}) %all-gather.5.cloned.1.call-update) | async-done | bytes 4194320 | tf_op jit(solution)/shard_map/all_gather | solution.py:65
  400.8 0.0 copy-done
  400.8 5.8 %convolution_convert_fusion.1 = bf16[2048,500]{0,1:T(8,128)(2,1)} fusion(bf16[2048,1024]{1,0:T(8,128)(2,1)} %all-gather.5.cloned.1.call-done, bf16[1024,500]{0,1:T(8,128)(2,1)S(1)} %copy-done), kind=kOutput, calls=%fused_computation.7 | convolution fusion | flops 2098176000 | bytes 7266304 | tf_op jit(solution)/shard_map/dot_general | solution.py:67
  406.6 0.0 reduce-scatter.5.cloned.1.call-update
  406.7 0.0 copy-done.2
  406.7 0.1 constant_dynamic-slice_fusion
  406.7 0.1 copy.22
  406.8 0.6 convert_reduce_fusion.1
  408.1 0.1 add_multiply_fusion
  408.2 0.1 copy.26
  408.2 27.4 %reduce-scatter.5.cloned.1.call-done = bf16[512,500]{0,1:T(8,128)(2,1)} async-done(((bf16[2048,500]{0,1:T(8,128)(2,1)}), bf16[512,500]{0,1:T(8,128)(2,1)}) %reduce-scatter.5.cloned.1.call-update) | async-done | bytes 512016 | tf_op jit(solution)/shard_map/reduce_scatter | solution.py:66
  435.6 1.4 maximum_log-plus-one_fusion
  437.1 0.3 copy.25
  437.4 0.5 add_divide_fusion
  437.9 0.7 reshape.46
  (4 shorter events, 0.1 us)
Async XLA Ops:
  6.5 394.3 %copy-start = (bf16[1024,500]{0,1:T(8,128)(2,1)S(1)}, bf16[1024,500]{0,1:T(8,128)(2,1)}, u32[]{:S(2)}) copy-start(bf16[1024,500]{0,1:T(8,128)(2,1)} %param.15) | copy-start | bytes 3072004
  6.5 149.7 %all-gather.3.cloned.1.call-start = ((), (), s32[]{:S(2)}) async-start(), calls=%async_computation.4 | async-start | bytes 10485760 | tf_op jit(solution)/shard_map/all_gather | solution.py:51
  72.8 190.5 %reduce-scatter.3.cloned.1.call-start = ((), (), s32[]{:S(2)}) async-start(), calls=%async_computation.5 | async-start | bytes 10485760 | tf_op jit(solution)/shard_map/reduce_scatter | solution.py:58
  179.1 95.0 %copy-start.4 = (f32[32,2]{0,1:T(2,128)S(1)}, f32[32,2]{0,1:T(2,128)}, u32[]{:S(2)}) copy-start(f32[32,2]{0,1:T(2,128)} %param.11) | copy-start | bytes 772
  179.1 144.9 %copy-start.1 = (bf16[32,1024]{1,0:T(8,128)(2,1)S(1)}, bf16[32,1024]{1,0:T(8,128)(2,1)}, u32[]{:S(2)}) copy-start(bf16[32,1024]{1,0:T(8,128)(2,1)} %param.9) | copy-start | bytes 196612
  263.4 60.3 %all-to-all-start.1 = ((bf16[64,16,1024]{2,1,0:T(8,128)(2,1)}), bf16[64,16,1024]{2,1,0:T(8,128)(2,1)S(1)}, u32[]{:S(2)}, u32[]{:S(2)}) async-start(bf16[64,16,1024]{2,1,0:T(8,128)(2,1)} %reduce-scatter.3.cloned.1.call-done), calls=%async_computation.2 | async-start | bytes 4194304 | tf_op jit(solution)/shard_map/all_to_all | solution.py:59
  274.0 126.8 %all-gather.5.cloned.1.call-start = ((), (), s32[]{:S(2)}) async-start(), calls=%async_computation.6 | async-start | bytes 4259840 | tf_op jit(solution)/shard_map/all_gather | solution.py:65
  325.1 81.6 %copy-start.2 = (s32[64,32]{0,1:T(8,128)S(1)}, s32[64,32]{0,1:T(8,128)}, u32[]{:S(2)}) copy-start(s32[64,32]{0,1:T(8,128)} %param.16) | copy-start | bytes 24580
  325.1 81.7 %copy-start.3 = (s32[64,4]{0,1:T(4,128)S(1)}, s32[64,4]{0,1:T(4,128)}, u32[]{:S(2)}) copy-start(s32[64,4]{0,1:T(4,128)} %param.17) | copy-start | bytes 3076
  325.1 110.5 %reduce-scatter.5.cloned.1.call-start = ((), (), s32[]{:S(2)}) async-start(), calls=%async_computation.7 | async-start | bytes 2580480 | tf_op jit(solution)/shard_map/reduce_scatter | solution.py:66
Sparse Core Ops, SparseCore 0:
  73.0 83.2 all-gather.2
  179.2 84.1 reduce-scatter.2
  325.2 75.5 all-gather.4
  406.8 28.8 reduce-scatter.4
where the time goes:
time: 445 us
  waiting for transfers between devices  320 us (72%)
  blocking collectives  62.7 us (14%)
  matrix products  31.2 us (7%)
  between operations  13.9 us (3%)
  starting transfers between devices  10.9 us (2%)
    reduce_scatter x1, waiting for transfers between devices, local(): lax.psum_scatter(rounded.astype(jnp.bfloat16), 'voc', scatter_dimension=2...  84.3 us
    all_gather x1, waiting for transfers between devices, local(): block_rows = lax.all_gather(received, 'voc', axis=1, tiled=True)  83.4 us
    all_gather x1, waiting for transfers between devices, local(): gathered = lax.all_gather(layer_out, 'exp', axis=0, tiled=True)  75.4 us
    all_to_all x1, blocking collectives, local(): lax.all_to_all(send_rows, 'exp', split_axis=0, concat_axis=0, tiled=True)  62.7 us
    all_to_all x1, waiting for transfers between devices, local(): lax.all_to_all(summed, 'exp', split_axis=0, concat_axis=0, tiled=True)  49.6 us
    reduce_scatter x1, waiting for transfers between devices, local(): lax.psum_scatter(jnp.dot(gathered, head_weight, preferred_element_type=jn...  27.4 us
    dot_general x1, matrix products, local(): part = jnp.dot(hidden, down_local, preferred_element_type=jnp.float32)  15.2 us
    all_to_all x1, starting transfers between devices, local(): lax.all_to_all(summed, 'exp', split_axis=0, concat_axis=0, tiled=True)  10.6 us
  transfers between devices with their start and end apart: 5, of which 5 were waited for; matrix products, arithmetic and copies ran while one was open for 0% of the time, Pallas kernels for 0%

commit v1 on v0

--- a/solution.py
+++ b/solution.py
@@ -48,7 +48,10 @@
     send_rows = build_slots(place_table, tokens, group_size)
     received = lax.all_to_all(send_rows, "exp", split_axis=0, concat_axis=0, tiled=True)
     received = received.reshape(slot_count, width_slice)
-    block_rows = lax.all_gather(received, "voc", axis=1, tiled=True)
+    count_2 = lax.axis_size("voc")
+    parts = jnp.stack([received for _ in range(count_2)])
+    parts = lax.all_to_all(parts, "voc", split_axis=0, concat_axis=0)
+    block_rows = jnp.concatenate(parts, axis=1)
     gate_pre = jnp.dot(block_rows, gate_local, preferred_element_type=jnp.float32)
     up_pre = jnp.dot(block_rows, up_local, preferred_element_type=jnp.float32)
     hidden = (jax.nn.silu(gate_pre) * up_pre).astype(jnp.bfloat16)

time: 445 us -> 460 us (1.034)
  blocking collectives: 62.7 us -> 158 us
  waiting for transfers between devices: 320 us -> 234 us
  local copies, waits for them, and re-layouts: 2.67 us -> 9.94 us
    all_to_all x0 -> x1, blocking collectives: none -> 95.4 us  [local(): parts = lax.all_to_all(parts, 'voc', split_axis=0, concat_axis=0)]
    all_gather x1 -> x0, waiting for transfers between devices: 83.4 us -> none  [local(): block_rows = lax.all_gather(received, 'voc', axis=1, tiled=True)]
  transfers between devices with their start and end apart: 5 -> 4, of which waited for: 5 -> 4; matrix products, arithmetic and copies ran while one was open for 0% -> 0% of each run, Pallas kernels for 0% -> 0%
where the time goes in v1:
time: 460 us
  waiting for transfers between devices  234 us (51%)
  blocking collectives  158 us (34%)
  matrix products  29 us (6%)
  between operations  13.9 us (3%)
  starting transfers between devices  10.9 us (2%)
  local copies, waits for them, and re-layouts  9.94 us (2%)
    all_to_all x1, blocking collectives, local(): parts = lax.all_to_all(parts, 'voc', split_axis=0, concat_axis=0)  95.4 us
    reduce_scatter x1, waiting for transfers between devices, local(): lax.psum_scatter(rounded.astype(jnp.bfloat16), 'voc', scatter_dimension=2...  81.7 us
    all_gather x1, waiting for transfers between devices, local(): gathered = lax.all_gather(layer_out, 'exp', axis=0, tiled=True)  75.4 us
    all_to_all x1, blocking collectives, local(): lax.all_to_all(send_rows, 'exp', split_axis=0, concat_axis=0, tiled=True)  62.7 us
    all_to_all x1, waiting for transfers between devices, local(): lax.all_to_all(summed, 'exp', split_axis=0, concat_axis=0, tiled=True)  49.6 us
    reduce_scatter x1, waiting for transfers between devices, local(): lax.psum_scatter(jnp.dot(gathered, head_weight, preferred_element_type=jn...  27.4 us
    dot_general x1, matrix products, local(): part = jnp.dot(hidden, down_local, preferred_element_type=jnp.float32)  15.4 us
    all_to_all x1, starting transfers between devices, local(): lax.all_to_all(summed, 'exp', split_axis=0, concat_axis=0, tiled=True)  10.6 us
  transfers between devices with their start and end apart: 4, of which 4 were waited for; matrix products, arithmetic and copies ran while one was open for 0% of the time, Pallas kernels for 0%

profile of v1, /device:TPU:1, one launch (start us, length us, event | category | flops | bytes accessed | tf_op | source)
XLA Modules:
  0.0 459.6 jit_solution(15644424020593487010)
XLA Ops:
  6.5 0.0 copy-start
  6.5 0.0 reduce-scatter.3.cloned.1.call-start
  6.5 0.8 copy.31
  7.4 0.7 fusion.20
  8.1 0.1 eq.65
  8.2 0.1 fusion.16
  8.2 0.1 reduce_window_sum.11
  8.3 0.2 select_reduce_fusion
  8.5 0.1 eq.69
  8.6 0.1 copy.32
  8.8 1.0 convolution_convert_fusion.2
  9.8 0.3 broadcast_in_dim.2
  10.1 62.7 %all_to_all.15 = bf16[64,16,1024]{2,1,0:T(8,128)(2,1)} all-to-all(bf16[64,16,1024]{2,1,0:T(8,128)(2,1)S(1)} %bitcast.42), channel_id=1, replica_groups=mesh['exp'=64,'voc'=4] {'exp'}, dimensions={0} | all-to-all | bytes 4194304 | tf_op jit(solution)/shard_map/all_to_all | solution.py:49
  72.8 2.9 copy.33
  75.7 1.2 stack.3
  76.9 0.0 copy-start.6
  76.9 95.4 %all_to_all.16 = bf16[4,1024,1024]{1,2,0:T(8,128)(2,1)S(1)} all-to-all(bf16[4,1024,1024]{1,2,0:T(8,128)(2,1)S(1)} %stack.3), channel_id=1, replica_groups=mesh['exp'=64,'voc'=4] {'voc'}, dimensions={0} | all-to-all | bytes 16777216 | tf_op jit(solution)/shard_map/all_to_all | solution.py:53
  172.3 3.2 copy-done.1
  175.5 0.0 copy-done.6
  175.5 5.2 %fusion.3 = f32[1024,448]{0,1:T(8,128)} fusion(bf16[1024,4096]{0,1:T(8,128)(2,1)S(1)} %bitcast.40, bf16[1,4096,448]{1,2,0:T(8,128)(2,1)S(1)} %copy-done.6), kind=kOutput, calls=%fused_computation.5 | convolution fusion | flops 3758096384 | bytes 13893632 | tf_op jit(solution)/shard_map/dot_general | solution.py:55
  180.7 15.4 %convolution_convert_fusion = bf16[1024,4096]{1,0:T(8,128)(2,1)} fusion(bf16[1,448,4096]{2,1,0:T(8,128)(2,1)} %param.14, f32[1024,448]{0,1:T(8,128)} %fusion.3, bf16[1024,4096]{0,1:T(8,128)(2,1)} %bitcast.41, bf16[1,4096,448]{1,2,0:T(8,128)(2,1)} %param.13), kind=kOutput, calls=%fused_computation | convolution fusion | flops 7523139584 | bytes 25952256 | tf_op jit(solution)/shard_map/dot_general | solution.py:58
  196.2 0.0 reduce-scatter.3.cloned.1.call-update
  196.2 0.0 copy-start.5
  196.2 0.0 copy-start.2
  196.2 81.7 %reduce-scatter.3.cloned.1.call-done = bf16[64,16,1024]{2,1,0:T(8,128)(2,1)} async-done(((bf16[64,16,4096]{2,1,0:T(8,128)(2,1)}), bf16[64,16,1024]{2,1,0:T(8,128)(2,1)}) %reduce-scatter.3.cloned.1.call-update) | async-done | bytes 2097168 | tf_op jit(solution)/shard_map/reduce_scatter | solution.py:61
  277.9 10.6 %all-to-all-start.2 = ((bf16[64,16,1024]{2,1,0:T(8,128)(2,1)}), bf16[64,16,1024]{2,1,0:T(8,128)(2,1)S(1)}, u32[]{:S(2)}, u32[]{:S(2)}) async-start(bf16[64,16,1024]{2,1,0:T(8,128)(2,1)} %reduce-scatter.3.cloned.1.call-done), calls=%async_computation.3 | async-start | bytes 4194304 | tf_op jit(solution)/shard_map/all_to_all | solution.py:62
  288.5 0.0 all-gather.2.cloned.1.call-start
  288.6 0.0 copy-done.5
  288.6 49.6 %all-to-all-done.2 = bf16[64,16,1024]{2,1,0:T(8,128)(2,1)S(1)} async-done(((bf16[64,16,1024]{2,1,0:T(8,128)(2,1)}), bf16[64,16,1024]{2,1,0:T(8,128)(2,1)S(1)}, u32[]{:S(2)}, u32[]{:S(2)}) %all-to-all-start.2) | async-done | bytes 2097184 | tf_op jit(solution)/shard_map/all_to_all | solution.py:62
  338.2 0.4 convert_reduce_fusion
  338.6 1.0 fusion.10
  339.6 0.0 all-gather.2.cloned.1.call-update
  339.6 0.0 copy-start.3
  339.6 0.0 copy-start.4
  339.6 0.2 reduce-scatter.5.cloned.1.call-start
  339.9 75.4 %all-gather.2.cloned.1.call-done = bf16[2048,1024]{1,0:T(8,128)(2,1)} async-done(((bf16[32,1024]{1,0:T(8,128)(2,1)}), bf16[2048,1024]{1,0:T(8,128)(2,1)}) %all-gather.2.cloned.1.call-update) | async-done | bytes 4194320 | tf_op jit(solution)/shard_map/all_gather | solution.py:68
  415.3 5.9 %convolution_convert_fusion.1 = bf16[2048,500]{0,1:T(8,128)(2,1)} fusion(bf16[2048,1024]{1,0:T(8,128)(2,1)} %all-gather.2.cloned.1.call-done, bf16[1024,500]{0,1:T(8,128)(2,1)S(1)} %copy-done), kind=kOutput, calls=%fused_computation.7 | convolution fusion | flops 2098176000 | bytes 7266304 | tf_op jit(solution)/shard_map/dot_general | solution.py:70
  421.2 0.0 reduce-scatter.5.cloned.1.call-update
  421.2 0.1 constant_dynamic-slice_fusion
  421.3 0.1 copy.30
  421.4 0.6 convert_reduce_fusion.1
  422.6 0.1 add_multiply_fusion
  422.7 0.1 copy.35
  422.8 27.4 %reduce-scatter.5.cloned.1.call-done = bf16[512,500]{0,1:T(8,128)(2,1)} async-done(((bf16[2048,500]{0,1:T(8,128)(2,1)}), bf16[512,500]{0,1:T(8,128)(2,1)}) %reduce-scatter.5.cloned.1.call-update) | async-done | bytes 512016 | tf_op jit(solution)/shard_map/reduce_scatter | solution.py:69
  450.2 1.4 maximum_log-plus-one_fusion
  451.6 0.3 copy.34
  451.9 0.5 add_divide_fusion
  452.4 0.7 reshape.52
  (8 shorter events, 0.1 us)
Async XLA Ops:
  6.5 408.8 %copy-start = (bf16[1024,500]{0,1:T(8,128)(2,1)S(1)}, bf16[1024,500]{0,1:T(8,128)(2,1)}, u32[]{:S(2)}) copy-start(bf16[1024,500]{0,1:T(8,128)(2,1)} %param.15) | copy-start | bytes 3072004
  6.5 271.3 %reduce-scatter.3.cloned.1.call-start = ((), (), s32[]{:S(2)}) async-start(), calls=%async_computation.5 | async-start | bytes 10485760 | tf_op jit(solution)/shard_map/reduce_scatter | solution.py:61
  76.9 98.7 %copy-start.6 = (bf16[1,4096,448]{1,2,0:T(8,128)(2,1)S(1)}, bf16[1,4096,448]{1,2,0:T(8,128)(2,1)}, u32[]{:S(2)}) copy-start(bf16[1,4096,448]{1,2,0:T(8,128)(2,1)} %param.12) | copy-start | bytes 11010052
  172.3 3.2 copy-start.1
  196.2 92.4 %copy-start.5 = (f32[32,2]{0,1:T(2,128)S(1)}, f32[32,2]{0,1:T(2,128)}, u32[]{:S(2)}) copy-start(f32[32,2]{0,1:T(2,128)} %param.11) | copy-start | bytes 772
  196.2 142.4 %copy-start.2 = (bf16[32,1024]{1,0:T(8,128)(2,1)S(1)}, bf16[32,1024]{1,0:T(8,128)(2,1)}, u32[]{:S(2)}) copy-start(bf16[32,1024]{1,0:T(8,128)(2,1)} %param.9) | copy-start | bytes 196612
  277.9 60.3 %all-to-all-start.2 = ((bf16[64,16,1024]{2,1,0:T(8,128)(2,1)}), bf16[64,16,1024]{2,1,0:T(8,128)(2,1)S(1)}, u32[]{:S(2)}, u32[]{:S(2)}) async-start(bf16[64,16,1024]{2,1,0:T(8,128)(2,1)} %reduce-scatter.3.cloned.1.call-done), calls=%async_computation.3 | async-start | bytes 4194304 | tf_op jit(solution)/shard_map/all_to_all | solution.py:62
  288.5 126.8 %all-gather.2.cloned.1.call-start = ((), (), s32[]{:S(2)}) async-start(), calls=%async_computation.6 | async-start | bytes 4259840 | tf_op jit(solution)/shard_map/all_gather | solution.py:68
  339.6 81.6 %copy-start.3 = (s32[64,32]{0,1:T(8,128)S(1)}, s32[64,32]{0,1:T(8,128)}, u32[]{:S(2)}) copy-start(s32[64,32]{0,1:T(8,128)} %param.16) | copy-start | bytes 24580
  339.6 81.7 %copy-start.4 = (s32[64,4]{0,1:T(4,128)S(1)}, s32[64,4]{0,1:T(4,128)}, u32[]{:S(2)}) copy-start(s32[64,4]{0,1:T(4,128)} %param.17) | copy-start | bytes 3076
  339.6 110.5 %reduce-scatter.5.cloned.1.call-start = ((), (), s32[]{:S(2)}) async-start(), calls=%async_computation.7 | async-start | bytes 2580480 | tf_op jit(solution)/shard_map/reduce_scatter | solution.py:69
Sparse Core Ops, SparseCore 0:
  196.3 81.5 reduce-scatter.2
  339.7 75.5 all-gather.1
  421.3 28.8 reduce-scatter.4
